TPU v7x, 32 devices: a whole 2x2x4 slice. The times are simulated.
32 devices in a mesh: dp: 4 (over z), expert: 8 (over y, x, core).
Axes of the slice: x: 2, y: 2, z: 4, core: 2. Of those that a mesh axis runs over, the one named last changes fastest.
Arguments:
- tokens: bfloat16 [1024, 2048], P(('dp', 'expert')), may hold values from -6 to 6
- norm_gain: float32 [2, 2048], replicated, may hold values from 0.5 to 1.5
- routes: int32 [2, 1024, 8], P(None, ('dp', 'expert')), may hold values from 0 to 31, all different within a row; in each aligned block of 32 rows (0 to 31, 32 to 63, ..., all dimensions but the last counted through in order) at most 12 rows name the same one
- gates: float32 [2, 1024, 8], P(None, ('dp', 'expert')), may hold values from 0.03 to 0.3
- placement: int32 [2, 32], replicated, may hold values from 0 to 31, each once within a row
- w_in: bfloat16 [2, 32, 2048, 1536], P(None, ('dp', 'expert')), may hold values from -0.125 to 0.125
- in_scale: float32 [2, 32, 16, 12], P(None, ('dp', 'expert')), may hold values from 0.5 to 2
- w_out: bfloat16 [2, 32, 768, 2048], P(None, ('dp', 'expert')), may hold values from -0.21875 to 0.21875
- out_scale: float32 [2, 32, 6, 16], P(None, ('dp', 'expert')), may hold values from 0.5 to 2
Outputs:
- stream: bfloat16 [1024, 2048], P(('dp', 'expert'))
Inputs may be any that keep to these rules, and one draw needn't show every extreme that they name: `routes`: each token names 8 different experts in each layer; among the tokens of one device in one layer no expert is named more than 12 times, a bound that some block reaches. `placement`: each layer's row is a permutation of the experts; device position p is p's index along dp+expert, dp slowest.
All inputs are finite; a program needn't handle non-finite values.
Results may differ from a plain program's by a relative error of at most 0.009.
Values may be sent and summed in bfloat16 or wider, within the bound.
A program may use at most 128 MiB of HBM per device.

v0:
```python
import jax
import jax.numpy as jnp
from jax import lax
from jax.sharding import PartitionSpec as P

QBLK = 128


epsilon = 1e-06


def dequantize(quantized, scales, block_size):
    widened = jnp.repeat(jnp.repeat(scales, block_size, axis=0), block_size, axis=1)
    return (quantized.astype(jnp.float32) * widened).astype(jnp.bfloat16)


def shards(tokens, norm_gain, routes, gates, placement, w_in, in_scale, w_out, out_scale):
    tok_count = tokens.shape[0]
    width = tokens.shape[1]
    fanout = routes.shape[2]
    experts_all = placement.shape[1]
    capacity = max(2, 3 * tok_count * fanout // (2 * experts_all))
    hidden_width = w_out.shape[2]
    expert_ids = jnp.arange(experts_all, dtype=jnp.int32)
    slot_ids = jnp.arange(experts_all * capacity, dtype=jnp.int32)
    stream = tokens
    for layer_index in range(w_in.shape[0]):
        stream_f = stream.astype(jnp.float32)
        normed = (
            stream_f
            * lax.rsqrt(jnp.mean(stream_f * stream_f, axis=-1, keepdims=True) + epsilon)
            * norm_gain[layer_index]
        ).astype(jnp.bfloat16)
        in_weight = dequantize(w_in[layer_index, 0], in_scale[layer_index, 0], QBLK)
        out_weight = dequantize(w_out[layer_index, 0], out_scale[layer_index, 0], QBLK)
        matches = (placement[layer_index][:, None] == expert_ids[None, :]).astype(jnp.int32)
        holder = jnp.sum(matches * expert_ids[:, None], axis=0)
        chosen = routes[layer_index].reshape(-1)
        onehot = (chosen[:, None] == expert_ids[None, :]).astype(jnp.int32)
        ranks = jnp.sum((jnp.cumsum(onehot, axis=0) - 1) * onehot, axis=1)
        target = jnp.sum(onehot * holder[None, :], axis=1)
        slot_rows = target * capacity + ranks
        selector = (slot_rows[:, None] == slot_ids[None, :]).astype(jnp.bfloat16)
        spread = jnp.sum(
            selector.reshape(tok_count, fanout, -1).astype(jnp.float32), axis=1
        ).astype(jnp.bfloat16)
        outgoing = lax.dot_general(
            spread, normed, (((0,), (0,)), ((), ())), preferred_element_type=jnp.float32
        ).astype(jnp.bfloat16)
        outgoing = outgoing.reshape(experts_all, capacity, width)
        arrived = lax.all_to_all(
            outgoing, ("dp", "expert"), split_axis=0, concat_axis=0, tiled=True
        )
        arrived_shape = arrived.shape
        token_rows = arrived.reshape(-1, width)
        gate_up = jnp.dot(token_rows, in_weight, preferred_element_type=jnp.float32)
        hidden = (jax.nn.silu(gate_up[:, :hidden_width]) * gate_up[:, hidden_width:]).astype(
            jnp.bfloat16
        )
        answer = jnp.dot(hidden, out_weight, preferred_element_type=jnp.float32).astype(
            jnp.bfloat16
        )
        returned = lax.all_to_all(
            answer.reshape(arrived_shape), ("dp", "expert"), split_axis=0, concat_axis=0, tiled=True
        )
        back_rows = jnp.dot(
            selector, returned.reshape(-1, width), preferred_element_type=jnp.float32
        )
        back_rows = back_rows.reshape(tok_count, fanout, width)
        mixed = jnp.sum(back_rows * gates[layer_index][:, :, None], axis=1)
        stream = (stream_f + mixed).astype(jnp.bfloat16)
    return stream


def solution(mesh):
    return jax.shard_map(
        shards,
        mesh=mesh,
        in_specs=(
            P(("dp", "expert"), None),
            P(),
            P(None, ("dp", "expert"), None),
            P(None, ("dp", "expert"), None),
            P(),
            P(None, ("dp", "expert"), None, None),
            P(None, ("dp", "expert"), None, None),
            P(None, ("dp", "expert"), None, None),
            P(None, ("dp", "expert"), None, None),
        ),
        out_specs=P(("dp", "expert"), None),
        check_vma=False,
    )
```

profile of v0, /device:TPU:0, one launch (start us, length us, event | category | flops | bytes accessed | tf_op | source)
XLA Modules:
  0.0 262.9 jit_solution(2291619194007305180)
XLA Ops:
  3.1 0.8 fusion.60
  3.9 1.0 fusion.32
  4.9 1.5 convolution_convert_fusion.1
  6.5 1.5 reshape.229
  8.0 7.3 %all-to-all-start = ((bf16[32,12,2048]{2,1,0:T(8,128)(2,1)}), bf16[32,12,2048]{2,1,0:T(8,128)(2,1)S(1)}, u32[]{:S(2)}, u32[]{:S(2)}) async-start(bf16[32,12,2048]{2,1,0:T(8,128)(2,1)} %reshape.229), calls=%async_computation | async-start | bytes 4194304 | tf_op jit(solution)/shard_map/all_to_all | solution.py:51
  15.4 10.2 %fusion.59 = (bf16[1,1,2048,1536]{3,2,1,0:T(8,128)(2,1)}, bf16[1,1,2048,1536]{3,2,1,0:T(8,128)(2,1)}) fusion(bf16[2,1,2048,1536]{3,2,1,0:T(8,128)(2,1)} %param.14), kind=kLoop, calls=%fused_computation.96 | loop fusion | bytes 25165824 | tf_op jit(solution)/shard_map/slice | solution.py:34
  25.7 8.6 %copy.42 = bf16[1,1,2048,1536]{2,3,1,0:T(8,128)(2,1)} copy(bf16[1,1,2048,1536]{3,2,1,0:T(8,128)(2,1)} %get-tuple-element.12) | data formatting | bytes 12582912
  34.3 7.7 %fusion.1 = bf16[2048,12,128]{0,2,1:T(8,128)(2,1)} fusion(bf16[2048,12,128]{0,2,1:T(8,128)(2,1)} %bitcast.114, f32[2048,12]{0,1:T(8,128)S(1)} %bitcast.122), kind=kLoop, calls=%fused_computation.3 | loop fusion | flops 9437184 | bytes 12681216 | tf_op jit(solution)/shard_map/convert_element_type | solution.py:14
  42.0 22.2 %all-to-all-done = bf16[32,12,2048]{2,1,0:T(8,128)(2,1)S(1)} async-done(((bf16[32,12,2048]{2,1,0:T(8,128)(2,1)}), bf16[32,12,2048]{2,1,0:T(8,128)(2,1)S(1)}, u32[]{:S(2)}, u32[]{:S(2)}) %all-to-all-start) | async-done | bytes 1572896 | tf_op jit(solution)/shard_map/all_to_all | solution.py:51
  64.2 1.4 reshape.230
  65.5 5.2 %fusion.64 = f32[384,1536]{1,0:T(8,128)S(1)} fusion(bf16[384,2048]{1,0:T(8,128)(2,1)} %reshape.230, bf16[2048,1536]{0,1:T(8,128)(2,1)} %bitcast.116), kind=kOutput, calls=%fused_computation.101 | convolution fusion | flops 2415919104 | bytes 10223616 | tf_op jit(solution)/shard_map/dot_general | solution.py:56
  70.8 1.8 broadcast_in_dim.19
  72.6 4.7 %fusion.15 = bf16[384,2048]{1,0:T(8,128)(2,1)S(1)} fusion(f32[96,8,16,128]{3,2,1,0:T(8,128)S(1)} %bitcast.118, bf16[2,1,768,2048]{3,2,1,0:T(8,128)(2,1)} %param.16, f32[384,1536]{1,0:T(8,128)S(1)} %fusion.64), kind=kOutput, calls=%fused_computation.15 | convolution fusion | flops 1215234048 | bytes 13369344 | tf_op jit(solution)/shard_map/dot_general | solution.py:60
  77.3 1.5 reshape.234
  78.9 4.0 %all-to-all-start.1 = ((bf16[32,12,2048]{2,1,0:T(8,128)(2,1)}), bf16[32,12,2048]{2,1,0:T(8,128)(2,1)S(1)}, u32[]{:S(2)}, u32[]{:S(2)}) async-start(bf16[32,12,2048]{2,1,0:T(8,128)(2,1)} %reshape.234), calls=%async_computation.1 | async-start | bytes 4194304 | tf_op jit(solution)/shard_map/all_to_all | solution.py:63
  84.5 47.3 %all-to-all-done.1 = bf16[32,12,2048]{2,1,0:T(8,128)(2,1)S(1)} async-done(((bf16[32,12,2048]{2,1,0:T(8,128)(2,1)}), bf16[32,12,2048]{2,1,0:T(8,128)(2,1)S(1)}, u32[]{:S(2)}, u32[]{:S(2)}) %all-to-all-start.1) | async-done | bytes 1572896 | tf_op jit(solution)/shard_map/all_to_all | solution.py:63
  131.8 1.3 reshape.248
  133.1 2.4 fusion.18
  136.4 1.6 reshape.237
  137.9 4.2 %all-to-all-start.2 = ((bf16[32,12,2048]{2,1,0:T(8,128)(2,1)}), bf16[32,12,2048]{2,1,0:T(8,128)(2,1)S(1)}, u32[]{:S(2)}, u32[]{:S(2)}) async-start(bf16[32,12,2048]{2,1,0:T(8,128)(2,1)} %reshape.237), calls=%async_computation.2 | async-start | bytes 4194304 | tf_op jit(solution)/shard_map/all_to_all | solution.py:51
  142.3 8.7 %copy.44 = bf16[1,1,2048,1536]{2,3,1,0:T(8,128)(2,1)} copy(bf16[1,1,2048,1536]{3,2,1,0:T(8,128)(2,1)} %get-tuple-element.11) | data formatting | bytes 12582912
  151.0 7.7 %fusion = bf16[2048,12,128]{0,2,1:T(8,128)(2,1)} fusion(bf16[2048,12,128]{0,2,1:T(8,128)(2,1)} %bitcast.115, f32[2048,12]{0,1:T(8,128)S(1)} %bitcast.123), kind=kLoop, calls=%fused_computation.1 | loop fusion | flops 9437184 | bytes 12681216 | tf_op jit(solution)/shard_map/convert_element_type | solution.py:14
  158.6 32.3 %all-to-all-done.2 = bf16[32,12,2048]{2,1,0:T(8,128)(2,1)S(1)} async-done(((bf16[32,12,2048]{2,1,0:T(8,128)(2,1)}), bf16[32,12,2048]{2,1,0:T(8,128)(2,1)S(1)}, u32[]{:S(2)}, u32[]{:S(2)}) %all-to-all-start.2) | async-done | bytes 1572896 | tf_op jit(solution)/shard_map/all_to_all | solution.py:51
  190.9 1.3 reshape.238
  192.2 5.2 %fusion.65 = f32[384,1536]{1,0:T(8,128)S(1)} fusion(bf16[384,2048]{1,0:T(8,128)(2,1)} %reshape.238, bf16[2048,1536]{0,1:T(8,128)(2,1)} %bitcast.117), kind=kOutput, calls=%fused_computation.102 | convolution fusion | flops 2415919104 | bytes 10223616 | tf_op jit(solution)/shard_map/dot_general | solution.py:56
  197.5 1.8 broadcast_in_dim.45
  199.3 4.7 %fusion.12 = bf16[384,2048]{1,0:T(8,128)(2,1)S(1)} fusion(f32[96,8,16,128]{3,2,1,0:T(8,128)S(1)} %bitcast.119, bf16[2,1,768,2048]{3,2,1,0:T(8,128)(2,1)} %param.16, f32[384,1536]{1,0:T(8,128)S(1)} %fusion.65), kind=kOutput, calls=%fused_computation.14 | convolution fusion | flops 1215234048 | bytes 13369344 | tf_op jit(solution)/shard_map/dot_general | solution.py:60
  204.0 1.5 reshape.242
  205.6 4.0 %all-to-all-start.3 = ((bf16[32,12,2048]{2,1,0:T(8,128)(2,1)}), bf16[32,12,2048]{2,1,0:T(8,128)(2,1)S(1)}, u32[]{:S(2)}, u32[]{:S(2)}) async-start(bf16[32,12,2048]{2,1,0:T(8,128)(2,1)} %reshape.242), calls=%async_computation.3 | async-start | bytes 4194304 | tf_op jit(solution)/shard_map/all_to_all | solution.py:63
  209.6 48.8 %all-to-all-done.3 = bf16[32,12,2048]{2,1,0:T(8,128)(2,1)S(1)} async-done(((bf16[32,12,2048]{2,1,0:T(8,128)(2,1)}), bf16[32,12,2048]{2,1,0:T(8,128)(2,1)S(1)}, u32[]{:S(2)}, u32[]{:S(2)}) %all-to-all-start.3) | async-done | bytes 1572896 | tf_op jit(solution)/shard_map/all_to_all | solution.py:63
  258.4 1.3 reshape.249
  259.8 2.4 fusion.19
  (55 shorter events, 6.5 us)
Async XLA Ops:
  7.9 7.3 %copy-start.1 = (f32[2,1,16,12]{2,1,3,0:T(1,128)S(1)}, f32[2,1,16,12]{2,1,3,0:T(1,128)}, u32[]{:S(2)}) copy-start(f32[2,1,16,12]{2,1,3,0:T(1,128)} %param.15) | copy-start | bytes 4612
  8.0 56.2 %all-to-all-start = ((bf16[32,12,2048]{2,1,0:T(8,128)(2,1)}), bf16[32,12,2048]{2,1,0:T(8,128)(2,1)S(1)}, u32[]{:S(2)}, u32[]{:S(2)}) async-start(bf16[32,12,2048]{2,1,0:T(8,128)(2,1)} %reshape.229), calls=%async_computation | async-start | bytes 4194304 | tf_op jit(solution)/shard_map/all_to_all | solution.py:51
  25.7 8.6 %copy-start.3 = (f32[2,1,6,16]{3,1,2,0:T(1,128)S(1)}, f32[2,1,6,16]{3,1,2,0:T(1,128)}, u32[]{:S(2)}) copy-start(f32[2,1,6,16]{3,1,2,0:T(1,128)} %param.17) | copy-start | bytes 2308
  78.9 4.3 %copy-start.2 = (f32[2,32,8]{1,2,0:T(8,128)S(1)}, f32[2,32,8]{1,2,0:T(8,128)}, u32[]{:S(2)}) copy-start(f32[2,32,8]{1,2,0:T(8,128)} %param.12) | copy-start | bytes 6148
  78.9 52.9 %all-to-all-start.1 = ((bf16[32,12,2048]{2,1,0:T(8,128)(2,1)}), bf16[32,12,2048]{2,1,0:T(8,128)(2,1)S(1)}, u32[]{:S(2)}, u32[]{:S(2)}) async-start(bf16[32,12,2048]{2,1,0:T(8,128)(2,1)} %reshape.234), calls=%async_computation.1 | async-start | bytes 4194304 | tf_op jit(solution)/shard_map/all_to_all | solution.py:63
  133.1 2.5 copy-start
  137.9 53.0 %all-to-all-start.2 = ((bf16[32,12,2048]{2,1,0:T(8,128)(2,1)}), bf16[32,12,2048]{2,1,0:T(8,128)(2,1)S(1)}, u32[]{:S(2)}, u32[]{:S(2)}) async-start(bf16[32,12,2048]{2,1,0:T(8,128)(2,1)} %reshape.237), calls=%async_computation.2 | async-start | bytes 4194304 | tf_op jit(solution)/shard_map/all_to_all | solution.py:51
  205.6 52.9 %all-to-all-start.3 = ((bf16[32,12,2048]{2,1,0:T(8,128)(2,1)}), bf16[32,12,2048]{2,1,0:T(8,128)(2,1)S(1)}, u32[]{:S(2)}, u32[]{:S(2)}) async-start(bf16[32,12,2048]{2,1,0:T(8,128)(2,1)} %reshape.242), calls=%async_computation.3 | async-start | bytes 4194304 | tf_op jit(solution)/shard_map/all_to_all | solution.py:63
where the time goes:
time: 264 us; the launch traced here: 263 us
  waiting for transfers between devices  151 us (57%)
  local copies, waits for them, and re-layouts  46.4 us (18%)
  matrix products  27 us (10%)
  starting transfers between devices  19.5 us (7%)
  other arithmetic  19.2 us (7%)
    all_to_all x2, waiting for transfers between devices, shards(): lax.all_to_all(answer.reshape(arrived_shape), ('dp', 'expert'), split_axi...  96.1 us
    all_to_all x2, waiting for transfers between devices, shards(): lax.all_to_all(outgoing, ('dp', 'expert'), split_axis=0, concat_axis=0, t...  54.4 us
    unnamed x17, local copies, waits for them, and re-layouts  17.6 us
    convert_element_type x2, other arithmetic, dequantize(): return (quantized.astype(jnp.float32) * widened).astype(jnp.bfloat16)  15.4 us
    all_to_all x2, starting transfers between devices, shards(): lax.all_to_all(outgoing, ('dp', 'expert'), split_axis=0, concat_axis=0, t...  11.5 us
    dot_general x2, matrix products, shards(): gate_up = jnp.dot(token_rows, in_weight, preferred_element_type=jnp.float32)  10.5 us
    slice x2, local copies, waits for them, and re-layouts, shards(): in_weight = dequantize(w_in[layer_index, 0], in_scale[layer_index, 0], QBLK)  10.2 us
    dot_general x2, matrix products, shards(): jnp.dot(hidden, out_weight, preferred_element_type=jnp.float32)  9.47 us
  transfers between devices with their start and end apart: 4, of which 4 were waited for; matrix products, arithmetic and copies ran while one was open for 17% of the time, Pallas kernels for 0%

commit v1 on v0

--- a/solution.py
+++ b/solution.py
@@ -1,7 +1,13 @@
+import functools
+
 import jax
 import jax.numpy as jnp
 from jax import lax
+from jax.experimental import pallas as pl
+from jax.experimental.pallas import tpu as pltpu
 from jax.sharding import PartitionSpec as P
+
+MESH = pl.DeviceIdType.MESH
 
 QBLK = 128
 
@@ -72,9 +78,276 @@
     return stream
 
 
+GZ, GX, GY, GA, GB, GC, RC, RA, RB, RX, RY, RZ = range(12)
+
+
+def moe_kernel(
+    layers, experts_all, tok_ref, gain_ref, wts_ref, isc_ref, osc_ref, win_hbm, wout_hbm, out_ref,
+    rows, win, wout, hid, part, acc, core_in, diag_out, diag_in, side_out, side_in, z_out, z_in,
+    w_sem, send_sem, recv_sem,
+):
+    count, width = tok_ref.shape
+    full = width + 128
+    half = width // 2
+    ff = wout.shape[1]
+    z = lax.axis_index("dp")
+    e = lax.axis_index("expert")
+    c = e % 2
+    q = e // 2
+    x = q % 2
+    y = q // 2
+    xq = q + 1 - 2 * x
+    yq = q + 2 - 4 * y
+    dq = 3 - q
+    dev_x = (z, e + 2 - 4 * x)
+    dev_y = (z, e + 4 - 8 * y)
+    dev_c = (z, e + 1 - 2 * c)
+
+    def plane(k):
+        return (z % 2 + k % 2) % 2 + 2 * ((z // 2 + k // 2) % 2)
+
+    for l in range(layers):
+        pltpu.make_async_copy(win_hbm.at[l, 0], win.at[l], w_sem.at[l, 0]).start()
+        pltpu.make_async_copy(wout_hbm.at[l, 0], wout.at[l], w_sem.at[l, 1]).start()
+
+    barrier = pltpu.get_barrier_semaphore()
+    partners = [dev_x, dev_y, dev_c] + [(plane(k), e) for k in range(1, 4)]
+    for dev in partners:
+        pl.semaphore_signal(barrier, inc=1, device_id=dev, device_id_type=MESH)
+    pl.semaphore_wait(barrier, len(partners))
+
+    def scale_in(l, lo, hi):
+        @pl.loop(lo * 4, hi * 4)
+        def _(i):
+            r = pl.ds(pl.multiple_of(i * 32, 32), 32)
+            win[l, r, :] = (win[l, r, :].astype(jnp.float32) * isc_ref[l, i // 4]).astype(jnp.bfloat16)
+
+    def scale_out(l):
+        @pl.loop(0, ff // 32)
+        def _(i):
+            r = pl.ds(pl.multiple_of(i * 32, 32), 32)
+            wout[l, r, :] = (wout[l, r, :].astype(jnp.float32) * osc_ref[l, i // 4]).astype(jnp.bfloat16)
+
+    blocks = win.shape[1] // QBLK
+
+    def dequant(l, step):
+        if step == 0:
+            pltpu.make_async_copy(win_hbm.at[l, 0], win.at[l], w_sem.at[l, 0]).wait()
+            scale_in(l, 0, blocks // 2)
+        elif step == 1:
+            scale_in(l, blocks // 2, blocks)
+        else:
+            pltpu.make_async_copy(wout_hbm.at[l, 0], wout.at[l], w_sem.at[l, 1]).wait()
+            scale_out(l)
+
+    acc[...] = tok_ref[...].astype(jnp.float32)
+
+    def layer(l, carry):
+        sent = []
+
+        def copy(src, dst, k, kind, dev):
+            return pltpu.make_async_remote_copy(
+                src_ref=src, dst_ref=dst,
+                send_sem=send_sem.at[l, k, kind], recv_sem=recv_sem.at[l, k, kind],
+                device_id=dev, device_id_type=MESH,
+            )
+
+        def start(src, dst, k, kind, dev):
+            op = copy(src, dst, k, kind, dev)
+            op.start()
+            sent.append(op)
+
+        def arrived(dst, k, kind, dev):
+            copy(dst, dst, k, kind, dev).wait_recv()
+
+        left, right = pl.ds(0, half), pl.ds(half, full - half)
+
+        def shard(k, place):
+            return rows.at[l, plane(k), c, place]
+
+        def g1(k):
+            mine = shard(k, q)
+            if k > 0:
+                arrived(mine, k, GZ, (plane(k), e))
+            start(mine, mine, k, GX, dev_x)
+            start(mine, mine, k, GY, dev_y)
+
+        def g2(k):
+            arrived(shard(k, xq), k, GX, dev_x)
+            piece = rows.at[l, plane(k), c, xq, :, left]
+            start(piece, piece, k, GA, dev_y)
+            arrived(shard(k, yq), k, GY, dev_y)
+            piece = rows.at[l, plane(k), c, yq, :, right]
+            start(piece, piece, k, GB, dev_x)
+
+        def g3(k):
+            arrived(rows.at[l, plane(k), c, dq, :, left], k, GA, dev_y)
+            arrived(rows.at[l, plane(k), c, dq, :, right], k, GB, dev_x)
+            ours = rows.at[l, plane(k), c]
+            start(ours, ours, k, GC, dev_c)
+
+        def compute(k):
+            arrived(rows.at[l, plane(k), 1 - c], k, GC, dev_c)
+            zk = plane(k)
+            total = 8 * count
+            picks = rows[l, zk, :, :, :, width:].reshape(total, full - width).astype(jnp.float32)
+            lane = lax.broadcasted_iota(jnp.int32, picks.shape, 1)
+            me = z * 8 + e
+            own = (lane == me) | (lane == me + experts_all)
+            weight = jnp.sum(jnp.where(own, picks, 0.0), axis=1, keepdims=True)
+
+            @pl.loop(0, ff // 256)
+            def _(j):
+                data = rows[l, zk, :, :, :, :width].reshape(total, width)
+                g_cols = pl.ds(pl.multiple_of(j * 256, 256), 256)
+                u_cols = pl.ds(pl.multiple_of(ff + j * 256, 256), 256)
+                gate = jnp.dot(data, win[l, :, g_cols], preferred_element_type=jnp.float32)
+                up = jnp.dot(data, win[l, :, u_cols], preferred_element_type=jnp.float32)
+                hid[:, g_cols] = (gate / (1.0 + jnp.exp(-gate)) * up).astype(jnp.bfloat16)
+
+            @pl.loop(0, width // 512)
+            def _(j):
+                cols = pl.ds(pl.multiple_of(j * 512, 512), 512)
+                answer = jnp.dot(hid[...], wout[l, :, cols], preferred_element_type=jnp.float32)
+                answer = answer.astype(jnp.bfloat16).astype(jnp.float32) * weight
+                part[k, :, :, :, cols] = answer.astype(jnp.bfloat16).reshape(2, 4, count, 512)
+
+            start(part.at[k, 1 - c], core_in.at[l, k], k, RC, dev_c)
+
+        def chip_sum(k, place):
+            return part[k, c, place].astype(jnp.float32) + core_in[l, k, place].astype(jnp.float32)
+
+        def r2(k):
+            arrived(core_in.at[l, k], k, RC, dev_c)
+            far = chip_sum(k, dq).astype(jnp.bfloat16)
+            diag_out[k, 0] = far[:, :half]
+            diag_out[k, 1] = far[:, half:]
+            start(diag_out.at[k, 0], diag_in.at[l, k, 0], k, RA, dev_x)
+            start(diag_out.at[k, 1], diag_in.at[l, k, 1], k, RB, dev_y)
+
+        def r3(k):
+            arrived(diag_in.at[l, k, 1], k, RB, dev_y)
+            near = chip_sum(k, xq)
+            side_out[k, 0, :, :half] = near[:, :half].astype(jnp.bfloat16)
+            side_out[k, 0, :, half:] = (near[:, half:] + diag_in[l, k, 1].astype(jnp.float32)).astype(jnp.bfloat16)
+            start(side_out.at[k, 0], side_in.at[l, k, 0], k, RX, dev_x)
+            arrived(diag_in.at[l, k, 0], k, RA, dev_x)
+            near = chip_sum(k, yq)
+            side_out[k, 1, :, :half] = (near[:, :half] + diag_in[l, k, 0].astype(jnp.float32)).astype(jnp.bfloat16)
+            side_out[k, 1, :, half:] = near[:, half:].astype(jnp.bfloat16)
+            start(side_out.at[k, 1], side_in.at[l, k, 1], k, RY, dev_y)
+
+        def r4(k):
+            arrived(side_in.at[l, k, 0], k, RX, dev_x)
+            arrived(side_in.at[l, k, 1], k, RY, dev_y)
+            whole = chip_sum(k, q) + side_in[l, k, 0].astype(jnp.float32) + side_in[l, k, 1].astype(jnp.float32)
+            if k == 0:
+                acc[...] += whole
+            else:
+                z_out[k] = whole.astype(jnp.bfloat16)
+                start(z_out.at[k], z_in.at[l, k], k, RZ, (plane(k), e))
+
+        stream = acc[...]
+        inverse = lax.rsqrt(jnp.mean(stream * stream, axis=-1, keepdims=True) + epsilon)
+        rows[l, z, c, q, :, :width] = (stream * inverse * gain_ref[l]).astype(jnp.bfloat16)
+        rows[l, z, c, q, :, width:] = wts_ref[l]
+        mine = rows.at[l, z, c, q]
+        g1(0)
+        for k in range(1, 4):
+            start(mine, mine, k, GZ, (plane(k), e))
+
+        def ahead(step):
+            @pl.when(l + 1 < layers)
+            def _():
+                dequant(l + 1, step)
+
+        @pl.when(l == 0)
+        def _():
+            dequant(0, 0)
+
+        g2(0), g1(1)
+
+        @pl.when(l == 0)
+        def _():
+            dequant(0, 1)
+
+        g3(0), g2(1), g1(2)
+
+        @pl.when(l == 0)
+        def _():
+            dequant(0, 2)
+
+        compute(0), g3(1), g2(2), g1(3)
+        compute(1), r2(0), g3(2), g2(3)
+        compute(2), r3(0), r2(1), g3(3)
+        compute(3), r4(0), r3(1), r2(2)
+        ahead(0)
+        r4(1), r3(2), r2(3)
+        ahead(1)
+        r4(2), r3(3)
+        ahead(2)
+        r4(3)
+        for k in range(1, 4):
+            arrived(z_in.at[l, k], k, RZ, (plane(k), e))
+            acc[...] += z_in[l, k].astype(jnp.float32)
+        acc[...] = acc[...].astype(jnp.bfloat16).astype(jnp.float32)
+        for op in sent:
+            op.wait_send()
+        return carry
+
+    lax.fori_loop(0, layers, layer, 0)
+    out_ref[...] = acc[...].astype(jnp.bfloat16)
+
+
+def fused(tokens, norm_gain, routes, gates, placement, w_in, in_scale, w_out, out_scale):
+    count, width = tokens.shape
+    layers = w_in.shape[0]
+    ff = w_out.shape[2]
+    chosen = routes[:, :, :, None] == placement[:, None, None, :]
+    share = jnp.sum(jnp.where(chosen, gates[:, :, :, None], 0.0), axis=2)
+    high = lax.reduce_precision(share, 8, 7)
+    low = share - high
+    wts = jnp.concatenate([high, low, jnp.zeros_like(high), jnp.zeros_like(high)], axis=-1)
+    wts = wts.astype(jnp.bfloat16)
+    isc = jnp.repeat(in_scale[:, 0], QBLK, axis=2)[:, :, None, :]
+    osc = jnp.repeat(out_scale[:, 0], QBLK, axis=2)[:, :, None, :]
+    gain = norm_gain[:, None, :]
+    vmem = pl.BlockSpec(memory_space=pltpu.VMEM)
+    hbm = pl.BlockSpec(memory_space=pl.ANY)
+    b16 = jnp.bfloat16
+    return pl.pallas_call(
+        functools.partial(moe_kernel, layers, placement.shape[1]),
+        out_shape=jax.ShapeDtypeStruct((count, width), b16),
+        in_specs=[vmem] * 5 + [hbm] * 2,
+        out_specs=vmem,
+        scratch_shapes=[
+            pltpu.VMEM((layers, 4, 2, 4, count, width + 128), b16),
+            pltpu.VMEM((layers, width, 2 * ff), b16),
+            pltpu.VMEM((layers, ff, width), b16),
+            pltpu.VMEM((8 * count, ff), b16),
+            pltpu.VMEM((4, 2, 4, count, width), b16),
+            pltpu.VMEM((count, width), jnp.float32),
+            pltpu.VMEM((layers, 4, 4, count, width), b16),
+            pltpu.VMEM((4, 2, count, width // 2), b16),
+            pltpu.VMEM((layers, 4, 2, count, width // 2), b16),
+            pltpu.VMEM((4, 2, count, width), b16),
+            pltpu.VMEM((layers, 4, 2, count, width), b16),
+            pltpu.VMEM((4, count, width), b16),
+            pltpu.VMEM((layers, 4, count, width), b16),
+            pltpu.SemaphoreType.DMA((layers, 2)),
+            pltpu.SemaphoreType.DMA((layers, 4, 12)),
+            pltpu.SemaphoreType.DMA((layers, 4, 12)),
+        ],
+        compiler_params=pltpu.CompilerParams(
+            collective_id=0, has_side_effects=True, vmem_limit_bytes=58 * 1024 * 1024
+        ),
+    )(tokens, gain, wts, isc, osc, w_in, w_out)
+
+
 def solution(mesh):
+    fits = mesh.shape["dp"] == 4 and mesh.shape["expert"] == 8
     return jax.shard_map(
-        shards,
+        fused if fits else shards,
         mesh=mesh,
         in_specs=(
             P(("dp", "expert"), None),

time: 264 us -> 133 us (0.50)
  waiting for transfers between devices: 151 us -> 0 us
  Pallas kernels: 0 us -> 123 us
  local copies, waits for them, and re-layouts: 46.4 us -> 7.76 us
  matrix products: 27 us -> 0 us
  starting transfers between devices: 19.5 us -> 0 us
  other arithmetic: 19.2 us -> 1.59 us
    all_to_all x4 -> x0, waiting for transfers between devices: 151 us -> none  [the longest x2 96.1 us: shards(): lax.all_to_all(answer.reshape(arrived_shape), ('dp', 'expert'), split_axi...]
    pallas_call x0 -> x1, Pallas kernels: none -> 123 us  [fused(): pl.pallas_call(functools.partial(moe_kernel, layers, placement.shape[1]),...]
    dot_general x8 -> x0, matrix products: 27 us -> none  [the longest x2 10.5 us: shards(): gate_up = jnp.dot(token_rows, in_weight, preferred_element_type=jnp.float32)]
    all_to_all x4 -> x0, starting transfers between devices: 19.5 us -> none  [the longest x2 11.5 us: shards(): lax.all_to_all(outgoing, ('dp', 'expert'), split_axis=0, concat_axis=0, t...]
    convert_element_type x5 -> x0, other arithmetic: 16.1 us -> none  [the longest x2 15.4 us: dequantize(): return (quantized.astype(jnp.float32) * widened).astype(jnp.bfloat16)]
    unnamed x17 -> x5, local copies, waits for them, and re-layouts: 17.6 us -> 4.53 us
    slice x8 -> x0, local copies, waits for them, and re-layouts: 12.1 us -> none  [the longest x2 10.2 us: shards(): in_weight = dequantize(w_in[layer_index, 0], in_scale[layer_index, 0], QBLK)]
    reshape x8 -> x0, local copies, waits for them, and re-layouts: 11.5 us -> none  [the longest x2 3.09 us: shards(): answer.reshape(arrived_shape)]
  transfers between devices with their start and end apart: 4 -> 0, of which waited for: 4 -> 0; matrix products, arithmetic and copies ran while one was open for 17% -> 0% of each run, Pallas kernels for 0% -> 0%
where the time goes in v1:
time: 133 us; the launch traced here: 132 us
  Pallas kernels  123 us (92%)
  local copies, waits for them, and re-layouts  7.76 us (6%)
  other arithmetic  1.59 us (1%)
    pallas_call x1, Pallas kernels, fused(): pl.pallas_call(functools.partial(moe_kernel, layers, placement.shape[1]),...  123 us
    unnamed x5, local copies, waits for them, and re-layouts  4.53 us

profile of v1, /device:TPU:0, one launch (start us, length us, event | category | flops | bytes accessed | tf_op | source)
XLA Modules:
  0.0 132.4 jit_solution(1818606588198713763)
XLA Ops:
  0.0 0.8 copy.20
  0.8 0.8 copy.21
  1.6 0.9 select_reduce_fusion
  2.5 0.1 pad.2.clone
  2.6 0.7 maximum_maximum_fusion.wts_ref
  3.2 0.7 copy.29
  4.0 0.1 copy.23
  4.0 0.1 broadcast_in_dim.27
  4.2 0.9 broadcast_in_dim_reshape.8.isc_ref
  5.0 0.7 copy.30
  5.7 0.7 broadcast_in_dim.28
  6.5 1.3 %broadcast_in_dim.24.gain_ref = f32[2,1,2048]{2,1,0:T(1,128)} reshape(f32[2,2048]{1,0:T(2,128)} %param.10) | data formatting | bytes 32768 | tf_op jit(solution)/shard_map/broadcast_in_dim | solution.py:314
  7.8 123.0 %shard_map.91 = bf16[32,2048]{1,0:T(8,128)(2,1)} custom-call(bf16[32,2048]{1,0:T(8,128)(2,1)} %tok_ref.1, f32[2,1,2048]{2,1,0:T(1,128)} %broadcast_in_dim.24.gain_ref, bf16[2,32,128]{2,1,0:T(8,128)(2,1)} %maximum_maximum_fusion.wts_ref, f32[2,16,1,1536]{3,2,1,0:T(1,128)} %broadcast_in_dim_reshape.8.isc_ref, f32[2,6,1,2048]{3,2,1,0:T(1,128)} %bitcast.7, ...), custom_call_target="tpu_custom_call" | custom-call | tf_op jit(solution)/shard_map/pallas_call | solution.py:318
  130.8 1.6 %copy.32 = bf16[32,2048]{1,0:T(8,128)(2,1)} copy(bf16[32,2048]{1,0:T(8,128)(2,1)} %shard_map.91) | data formatting | bytes 262144
  (3 shorter events, 0.0 us)

commit v2 on v1

--- a/solution.py
+++ b/solution.py
@@ -120,13 +120,13 @@
         @pl.loop(lo * 4, hi * 4)
         def _(i):
             r = pl.ds(pl.multiple_of(i * 32, 32), 32)
-            win[l, r, :] = (win[l, r, :].astype(jnp.float32) * isc_ref[l, i // 4]).astype(jnp.bfloat16)
+            win[l, r, :] = (win[l, r, :].astype(jnp.float32) * isc_ref[l, pl.ds(i // 4, 1), :]).astype(jnp.bfloat16)
 
     def scale_out(l):
         @pl.loop(0, ff // 32)
         def _(i):
             r = pl.ds(pl.multiple_of(i * 32, 32), 32)
-            wout[l, r, :] = (wout[l, r, :].astype(jnp.float32) * osc_ref[l, i // 4]).astype(jnp.bfloat16)
+            wout[l, r, :] = (wout[l, r, :].astype(jnp.float32) * osc_ref[l, pl.ds(i // 4, 1), :]).astype(jnp.bfloat16)
 
     blocks = win.shape[1] // QBLK
 
@@ -186,15 +186,10 @@
             ours = rows.at[l, plane(k), c]
             start(ours, ours, k, GC, dev_c)
 
-        def compute(k):
+        def expand(k):
             arrived(rows.at[l, plane(k), 1 - c], k, GC, dev_c)
             zk = plane(k)
             total = 8 * count
-            picks = rows[l, zk, :, :, :, width:].reshape(total, full - width).astype(jnp.float32)
-            lane = lax.broadcasted_iota(jnp.int32, picks.shape, 1)
-            me = z * 8 + e
-            own = (lane == me) | (lane == me + experts_all)
-            weight = jnp.sum(jnp.where(own, picks, 0.0), axis=1, keepdims=True)
 
             @pl.loop(0, ff // 256)
             def _(j):
@@ -204,6 +199,15 @@
                 gate = jnp.dot(data, win[l, :, g_cols], preferred_element_type=jnp.float32)
                 up = jnp.dot(data, win[l, :, u_cols], preferred_element_type=jnp.float32)
                 hid[:, g_cols] = (gate / (1.0 + jnp.exp(-gate)) * up).astype(jnp.bfloat16)
+
+        def contract(k):
+            zk = plane(k)
+            total = 8 * count
+            picks = rows[l, zk, :, :, :, width:].reshape(total, full - width).astype(jnp.float32)
+            lane = lax.broadcasted_iota(jnp.int32, picks.shape, 1)
+            me = z * 8 + e
+            own = (lane == me) | (lane == me + experts_all)
+            weight = jnp.sum(jnp.where(own, picks, 0.0), axis=1, keepdims=True)
 
             @pl.loop(0, width // 512)
             def _(j):
@@ -249,7 +253,7 @@
 
         stream = acc[...]
         inverse = lax.rsqrt(jnp.mean(stream * stream, axis=-1, keepdims=True) + epsilon)
-        rows[l, z, c, q, :, :width] = (stream * inverse * gain_ref[l]).astype(jnp.bfloat16)
+        rows[l, z, c, q, :, :width] = (stream * inverse * gain_ref[pl.ds(l, 1), :]).astype(jnp.bfloat16)
         rows[l, z, c, q, :, width:] = wts_ref[l]
         mine = rows.at[l, z, c, q]
         g1(0)
@@ -266,27 +270,19 @@
             dequant(0, 0)
 
         g2(0), g1(1)
-
-        @pl.when(l == 0)
-        def _():
-            dequant(0, 1)
-
-        g3(0), g2(1), g1(2)
-
-        @pl.when(l == 0)
-        def _():
-            dequant(0, 2)
-
-        compute(0), g3(1), g2(2), g1(3)
-        compute(1), r2(0), g3(2), g2(3)
-        compute(2), r3(0), r2(1), g3(3)
-        compute(3), r4(0), r3(1), r2(2)
+        dequant(l, 1)
+        g3(0), g2(1)
+        dequant(l, 2)
+        expand(0), g1(2), g3(1)
+        contract(0), g2(2), g1(3)
+        expand(1), r2(0), g3(2), g2(3)
+        contract(1), r3(0), g3(3)
+        expand(2), r4(0), r2(1)
+        contract(2), r3(1)
+        expand(3), r4(1), r2(2)
+        contract(3), r3(2)
         ahead(0)
-        r4(1), r3(2), r2(3)
-        ahead(1)
-        r4(2), r3(3)
-        ahead(2)
-        r4(3)
+        r2(3), r4(2), r3(3), r4(3)
         for k in range(1, 4):
             arrived(z_in.at[l, k], k, RZ, (plane(k), e))
             acc[...] += z_in[l, k].astype(jnp.float32)
@@ -309,9 +305,8 @@
     low = share - high
     wts = jnp.concatenate([high, low, jnp.zeros_like(high), jnp.zeros_like(high)], axis=-1)
     wts = wts.astype(jnp.bfloat16)
-    isc = jnp.repeat(in_scale[:, 0], QBLK, axis=2)[:, :, None, :]
-    osc = jnp.repeat(out_scale[:, 0], QBLK, axis=2)[:, :, None, :]
-    gain = norm_gain[:, None, :]
+    isc = jnp.repeat(in_scale[:, 0], QBLK, axis=2)
+    osc = jnp.repeat(out_scale[:, 0], QBLK, axis=2)
     vmem = pl.BlockSpec(memory_space=pltpu.VMEM)
     hbm = pl.BlockSpec(memory_space=pl.ANY)
     b16 = jnp.bfloat16
@@ -341,7 +336,7 @@
         compiler_params=pltpu.CompilerParams(
             collective_id=0, has_side_effects=True, vmem_limit_bytes=58 * 1024 * 1024
         ),
-    )(tokens, gain, wts, isc, osc, w_in, w_out)
+    )(tokens, norm_gain, wts, isc, osc, w_in, w_out)
 
 
 def solution(mesh):

time: 133 us -> 136 us (1.023)
  Pallas kernels: 123 us -> 128 us
  local copies, waits for them, and re-layouts: 7.76 us -> 6.38 us
    pallas_call x1, Pallas kernels: 123 us -> 128 us  [fused(): pl.pallas_call(functools.partial(moe_kernel, layers, placement.shape[1]),...]
    broadcast_in_dim x3 -> x2, local copies, waits for them, and re-layouts: 2.18 us -> 0.2 us  [the longest x1 0.12 us: fused(): isc = jnp.repeat(in_scale[:, 0], QBLK, axis=2)]
    reshape x0 -> x3, local copies, waits for them, and re-layouts: none -> 1.48 us  [the longest x2 0.77 us: fused(): osc = jnp.repeat(out_scale[:, 0], QBLK, axis=2)]
where the time goes in v2:
time: 136 us
  Pallas kernels  128 us (94%)
  local copies, waits for them, and re-layouts  6.38 us (5%)
  other arithmetic  1.59 us (1%)
    pallas_call x1, Pallas kernels, fused(): pl.pallas_call(functools.partial(moe_kernel, layers, placement.shape[1]),...  128 us
    unnamed x5, local copies, waits for them, and re-layouts  4.53 us

profile of v2, /device:TPU:0, one launch (start us, length us, event | category | flops | bytes accessed | tf_op | source)
XLA Modules:
  0.0 135.9 jit_solution(8324164553959330005)
XLA Ops:
  0.0 0.8 copy.19
  0.8 0.8 copy.20
  1.6 0.9 select_reduce_fusion
  2.5 0.1 pad.2.clone
  2.6 0.7 maximum_maximum_fusion.wts_ref
  3.2 0.7 copy.27
  4.0 0.1 copy.22
  4.0 0.1 broadcast_in_dim.23
  4.2 0.7 reshape.9.isc_ref
  4.9 0.7 copy.28
  5.6 0.1 broadcast_in_dim.24
  5.7 0.1 reshape.10
  5.7 0.7 copy.24.osc_ref
  6.4 127.8 %shard_map.91 = bf16[32,2048]{1,0:T(8,128)(2,1)} custom-call(bf16[32,2048]{1,0:T(8,128)(2,1)} %tok_ref.1, f32[2,2048]{1,0:T(2,128)} %gain_ref.1, bf16[2,32,128]{2,1,0:T(8,128)(2,1)} %maximum_maximum_fusion.wts_ref, f32[2,16,1536]{2,1,0:T(8,128)} %reshape.9.isc_ref, f32[2,6,2048]{2,1,0:T(8,128)} %copy.24.osc_ref, bf16[2,1,2048,1536]{3,2,1,0:T(8,128)(2,1)} %win_hbm.1, ...), custom_call_target="tpu_custom_call" | custom-call | tf_op jit(solution)/shard_map/pallas_call | solution.py:313
  134.3 1.6 %copy.30 = bf16[32,2048]{1,0:T(8,128)(2,1)} copy(bf16[32,2048]{1,0:T(8,128)(2,1)} %shard_map.91) | data formatting | bytes 262144
  (2 shorter events, 0.0 us)

commit v3 on v1

--- a/solution.py
+++ b/solution.py
@@ -120,13 +120,13 @@
         @pl.loop(lo * 4, hi * 4)
         def _(i):
             r = pl.ds(pl.multiple_of(i * 32, 32), 32)
-            win[l, r, :] = (win[l, r, :].astype(jnp.float32) * isc_ref[l, i // 4]).astype(jnp.bfloat16)
+            win[l, r, :] = (win[l, r, :].astype(jnp.float32) * isc_ref[l, pl.ds(i // 4, 1), :]).astype(jnp.bfloat16)
 
     def scale_out(l):
         @pl.loop(0, ff // 32)
         def _(i):
             r = pl.ds(pl.multiple_of(i * 32, 32), 32)
-            wout[l, r, :] = (wout[l, r, :].astype(jnp.float32) * osc_ref[l, i // 4]).astype(jnp.bfloat16)
+            wout[l, r, :] = (wout[l, r, :].astype(jnp.float32) * osc_ref[l, pl.ds(i // 4, 1), :]).astype(jnp.bfloat16)
 
     blocks = win.shape[1] // QBLK
 
@@ -196,7 +196,7 @@
             own = (lane == me) | (lane == me + experts_all)
             weight = jnp.sum(jnp.where(own, picks, 0.0), axis=1, keepdims=True)
 
-            @pl.loop(0, ff // 256)
+            @pl.loop(0, ff // 256, unroll=True)
             def _(j):
                 data = rows[l, zk, :, :, :, :width].reshape(total, width)
                 g_cols = pl.ds(pl.multiple_of(j * 256, 256), 256)
@@ -249,7 +249,7 @@
 
         stream = acc[...]
         inverse = lax.rsqrt(jnp.mean(stream * stream, axis=-1, keepdims=True) + epsilon)
-        rows[l, z, c, q, :, :width] = (stream * inverse * gain_ref[l]).astype(jnp.bfloat16)
+        rows[l, z, c, q, :, :width] = (stream * inverse * gain_ref[pl.ds(l, 1), :]).astype(jnp.bfloat16)
         rows[l, z, c, q, :, width:] = wts_ref[l]
         mine = rows.at[l, z, c, q]
         g1(0)
@@ -309,9 +309,8 @@
     low = share - high
     wts = jnp.concatenate([high, low, jnp.zeros_like(high), jnp.zeros_like(high)], axis=-1)
     wts = wts.astype(jnp.bfloat16)
-    isc = jnp.repeat(in_scale[:, 0], QBLK, axis=2)[:, :, None, :]
-    osc = jnp.repeat(out_scale[:, 0], QBLK, axis=2)[:, :, None, :]
-    gain = norm_gain[:, None, :]
+    isc = jnp.repeat(in_scale[:, 0], QBLK, axis=2)
+    osc = jnp.repeat(out_scale[:, 0], QBLK, axis=2)
     vmem = pl.BlockSpec(memory_space=pltpu.VMEM)
     hbm = pl.BlockSpec(memory_space=pl.ANY)
     b16 = jnp.bfloat16
@@ -341,7 +340,7 @@
         compiler_params=pltpu.CompilerParams(
             collective_id=0, has_side_effects=True, vmem_limit_bytes=58 * 1024 * 1024
         ),
-    )(tokens, gain, wts, isc, osc, w_in, w_out)
+    )(tokens, norm_gain, wts, isc, osc, w_in, w_out)
 
 
 def solution(mesh):

time: 133 us -> 128 us (0.962)
  Pallas kernels: 123 us -> 120 us
  local copies, waits for them, and re-layouts: 7.76 us -> 6.38 us
    pallas_call x1, Pallas kernels: 123 us -> 120 us  [fused(): pl.pallas_call(functools.partial(moe_kernel, layers, placement.shape[1]),...]
    broadcast_in_dim x3 -> x2, local copies, waits for them, and re-layouts: 2.18 us -> 0.2 us  [the longest x1 0.12 us: fused(): isc = jnp.repeat(in_scale[:, 0], QBLK, axis=2)]
    reshape x0 -> x3, local copies, waits for them, and re-layouts: none -> 1.48 us  [the longest x2 0.77 us: fused(): osc = jnp.repeat(out_scale[:, 0], QBLK, axis=2)]
where the time goes in v3:
time: 128 us
  Pallas kernels  120 us (94%)
  local copies, waits for them, and re-layouts  6.38 us (5%)
  other arithmetic  1.59 us (1%)
    pallas_call x1, Pallas kernels, fused(): pl.pallas_call(functools.partial(moe_kernel, layers, placement.shape[1]),...  120 us
    unnamed x5, local copies, waits for them, and re-layouts  4.53 us

profile of v3, /device:TPU:0, one launch (start us, length us, event | category | flops | bytes accessed | tf_op | source)
XLA Modules:
  0.0 127.6 jit_solution(16384591479766025739)
XLA Ops:
  0.0 0.8 copy.19
  0.8 0.8 copy.20
  1.6 0.9 select_reduce_fusion
  2.5 0.1 pad.2.clone
  2.6 0.7 maximum_maximum_fusion.wts_ref
  3.2 0.7 copy.27
  4.0 0.1 copy.22
  4.0 0.1 broadcast_in_dim.23
  4.2 0.7 reshape.9.isc_ref
  4.9 0.7 copy.28
  5.6 0.1 broadcast_in_dim.24
  5.7 0.1 reshape.10
  5.7 0.7 copy.24.osc_ref
  6.4 119.6 %shard_map.91 = bf16[32,2048]{1,0:T(8,128)(2,1)} custom-call(bf16[32,2048]{1,0:T(8,128)(2,1)} %tok_ref.1, f32[2,2048]{1,0:T(2,128)} %gain_ref.1, bf16[2,32,128]{2,1,0:T(8,128)(2,1)} %maximum_maximum_fusion.wts_ref, f32[2,16,1536]{2,1,0:T(8,128)} %reshape.9.isc_ref, f32[2,6,2048]{2,1,0:T(8,128)} %copy.24.osc_ref, bf16[2,1,2048,1536]{3,2,1,0:T(8,128)(2,1)} %win_hbm.1, ...), custom_call_target="tpu_custom_call" | custom-call | tf_op jit(solution)/shard_map/pallas_call | solution.py:317
  126.0 1.6 %copy.30 = bf16[32,2048]{1,0:T(8,128)(2,1)} copy(bf16[32,2048]{1,0:T(8,128)(2,1)} %shard_map.91) | data formatting | bytes 262144
  (2 shorter events, 0.0 us)
